TPU v7x, 512 devices: a whole 4x8x8 slice. The times are simulated.
512 devices in a mesh: row: 32 (over y, x), col: 16 (over z, core).
Axes of the slice: x: 4, y: 8, z: 8, core: 2. Of those that a mesh axis runs over, the one named last changes fastest.
Arguments:
- panel: float32 [1048576, 128], P(('row', 'col')), may hold values from -400 to 400
- next_panel: float32 [1048576, 128], P(('row', 'col')), may hold values from -600 to 600
Outputs:
- q_panel: float32 [1048576, 128], P(('row', 'col'))
- r_factor: float32 [128, 128], replicated
- coupling: float32 [128, 128], replicated
- trailing: float32 [1048576, 128], P(('row', 'col'))
All inputs are finite; a program needn't handle non-finite values.
Results may differ from a plain program's by a relative error of at most 0.00075.
Values sent between devices are 32-bit elements; how exact they have to be, the bound alone decides.
A program may use at most 64 MiB of HBM per device.

v0:
```python
import jax
import jax.numpy as jnp
from jax import lax
from jax.sharding import PartitionSpec as P


def factor(gram):
    eye = jnp.eye(gram.shape[0], dtype=gram.dtype)
    lower = jnp.linalg.cholesky(gram)
    lower_inv = lax.linalg.triangular_solve(lower, eye, left_side=True, lower=True)
    return (lower.T, lower_inv.T)


def inner(left, right):
    return jnp.einsum("rp,rq->pq", left, right, precision=lax.Precision.HIGHEST)


def times(left, right):
    return jnp.dot(left, right, precision=lax.Precision.HIGHEST)


def combine(stacked):
    return lax.psum(stacked, ("row", "col"))


def shards(panel, next_panel):
    count = panel.shape[0] * lax.axis_size("row") * lax.axis_size("col")
    gram_first = combine(inner(panel, panel)[None])[0] / count
    first_r, first_inv = factor(gram_first)
    draft = times(panel, first_inv)
    gram_second = combine(inner(draft, draft)[None])[0] / count
    second_r, second_inv = factor(gram_second)
    q_panel = times(draft, second_inv)
    r_factor = times(second_r, first_r)
    coupling = combine(inner(q_panel, next_panel)[None])[0] / count
    trailing = next_panel - times(q_panel, coupling)
    return (q_panel, r_factor, coupling, trailing)


def solution(mesh):
    return jax.shard_map(
        shards,
        mesh=mesh,
        in_specs=(P(("row", "col"), None), P(("row", "col"), None)),
        out_specs=(P(("row", "col"), None), P(), P(), P(("row", "col"), None)),
        check_vma=False,
    )
```

profile of v0, /device:TPU:1, one launch (start us, length us, event | category | flops | bytes accessed | tf_op | source)
XLA Modules:
  0.0 847.7 jit_solution(16755966553184550931)
XLA Ops:
  7.2 1.2 copy-done
  8.4 2.4 convolution_bitcast_fusion.2
  10.9 0.0 all-reduce.6.cloned.1.call-start
  10.9 267.1 %all-reduce.4.cloned.1.call-done = f32[1,128,128]{1,2,0:T(8,128)} async-done(((f32[1,128,128]{1,2,0:T(8,128)}), f32[1,128,128]{1,2,0:T(8,128)}) %all-reduce.4.cloned.1.call-update) | async-done | bytes 65552 | tf_op jit(solution)/shard_map/psum | solution.py:23
  278.0 0.8 multiply_bitcast_fusion.2
  278.9 0.1 copy.7
  279.0 0.7 copy-done.5
  279.7 11.7 %cholesky.44 = f32[128,128]{1,0:T(8,128)S(1)} custom-call(f32[128,128]{1,0:T(8,128)S(1)} %fusion.5), custom_call_target="Cholesky" | custom-call | tf_op jit(solution)/shard_map/jit(cholesky)/cholesky | solution.py:9
  291.5 0.6 compare_reduce_fusion.1
  292.1 0.7 select_bitcast_fusion.1
  292.8 9.8 %custom-call.6 = f32[1,128,128]{1,2,0:T(8,128)S(1)} custom-call(f32[1,128,128]{2,1,0:T(8,128)S(1)} %select_bitcast_fusion.1), custom_call_target="InvertDiagBlocksLowerTriangular" | custom-call | tf_op jit(solution)/shard_map/triangular_solve/custom-call.0 | solution.py:10
  302.6 0.3 fusion.2
  302.9 1.0 fusion.17
  303.9 1.6 convolution_bitcast_fusion.1
  305.6 0.2 all-reduce.8.cloned.1.call-start
  305.8 251.1 %all-reduce.6.cloned.1.call-done = f32[1,128,128]{1,2,0:T(8,128)} async-done(((f32[1,128,128]{1,2,0:T(8,128)}), f32[1,128,128]{1,2,0:T(8,128)}) %all-reduce.6.cloned.1.call-update) | async-done | bytes 65552 | tf_op jit(solution)/shard_map/psum | solution.py:23
  556.9 0.8 multiply_bitcast_fusion.1
  557.8 0.1 copy.9
  557.9 0.7 copy-done.6
  558.6 11.7 %cholesky.55 = f32[128,128]{1,0:T(8,128)S(1)} custom-call(f32[128,128]{1,0:T(8,128)S(1)} %fusion.4), custom_call_target="Cholesky" | custom-call | tf_op jit(solution)/shard_map/jit(cholesky)/cholesky | solution.py:9
  570.4 0.7 compare_reduce_fusion
  571.1 0.6 select_bitcast_fusion
  571.7 9.8 %custom-call.7 = f32[1,128,128]{1,2,0:T(8,128)S(1)} custom-call(f32[1,128,128]{2,1,0:T(8,128)S(1)} %select_bitcast_fusion), custom_call_target="InvertDiagBlocksLowerTriangular" | custom-call | tf_op jit(solution)/shard_map/triangular_solve/custom-call.0 | solution.py:10
  581.5 0.3 fusion
  581.8 1.8 fusion.18
  583.7 2.5 convolution_bitcast_fusion
  586.1 2.2 fusion.9
  588.3 249.2 %all-reduce.8.cloned.1.call-done = f32[1,128,128]{1,2,0:T(8,128)} async-done(((f32[1,128,128]{1,2,0:T(8,128)}), f32[1,128,128]{1,2,0:T(8,128)}) %all-reduce.8.cloned.1.call-update) | async-done | bytes 65552 | tf_op jit(solution)/shard_map/psum | solution.py:23
  837.5 0.8 multiply_bitcast_fusion
  838.4 0.7 copy.11
  839.1 0.1 copy-done.4
  839.2 2.0 convolution_subtract_fusion
  (18 shorter events, 0.2 us)
Async XLA Ops:
  7.2 1.2 copy-start
  7.2 270.9 %all-reduce.4.cloned.1.call-start = ((), (), s32[]{:S(2)}) async-start(), calls=%async_computation | async-start | bytes 131072 | tf_op jit(solution)/shard_map/psum | solution.py:23
  10.9 546.1 %all-reduce.6.cloned.1.call-start = ((), (), s32[]{:S(2)}) async-start(), calls=%async_computation.1 | async-start | bytes 131072 | tf_op jit(solution)/shard_map/psum | solution.py:23
  278.9 0.8 copy-start.5
  305.6 531.9 %all-reduce.8.cloned.1.call-start = ((), (), s32[]{:S(2)}) async-start(), calls=%async_computation.2 | async-start | bytes 131072 | tf_op jit(solution)/shard_map/psum | solution.py:23
  557.8 0.8 copy-start.6
  581.8 1.8 copy-start.2
  583.6 255.5 %copy-start.1 = (f32[2048,128]{1,0:T(8,128)}, f32[2048,128]{1,0:T(8,128)S(1)}, u32[]{:S(2)}) copy-start(f32[2048,128]{1,0:T(8,128)S(1)} %fusion.18) | copy-start | bytes 3145732
  583.6 255.5 %copy-start.3 = (f32[2048,128]{1,0:T(8,128)S(1)}, f32[2048,128]{1,0:T(8,128)}, u32[]{:S(2)}) copy-start(f32[2048,128]{1,0:T(8,128)} %param.6) | copy-start | bytes 3145732
  838.4 0.8 copy-start.4
Sparse Core Ops, SparseCore 0:
  13.6 264.4 all-reduce.3
  305.7 251.2 all-reduce.5
  586.3 251.2 all-reduce.7
where the time goes:
time: 848 us
  waiting for transfers between devices  768 us (91%)
  other arithmetic  48.3 us (6%)
  matrix products  14 us (2%)
  between operations  13.9 us (2%)
    psum x3, waiting for transfers between devices, combine(): return lax.psum(stacked, ('row', 'col'))  767 us
    another operation x6, other arithmetic, factor(): lower = jnp.linalg.cholesky(gram)  24.8 us
    another operation x4, other arithmetic, factor(): lax.linalg.triangular_solve(lower, eye, left_side=True, lower=True)  20.9 us
  transfers between devices with their start and end apart: 3, of which 3 were waited for; matrix products, arithmetic and copies ran while one was open for 0% of the time, Pallas kernels for 0%

commit v1 on v0

v1 whole, which is shorter than its diff:
```python
import functools

import jax
import jax.numpy as jnp
from jax import lax
from jax.experimental import pallas as pl
from jax.experimental.pallas import tpu as pltpu
from jax.sharding import PartitionSpec as P

MESH = pl.DeviceIdType.MESH
F32 = jnp.float32
BF16 = jnp.bfloat16
HIGHEST = lax.Precision.HIGHEST
N = 128
T = N // 8
HALF = T // 2
ROW_X = 4
ROW_Y = 8
COL_K = 2
COL_Z = 8
CHUNKS = ROW_X * COL_K
HI, LO, CO, DG, USED, PADDED = 0, 8, 16, 32, 34, 40


def two_sum(a, b):
    s = a + b
    t = s - a
    return s, (a - (s - t)) + (b - t)


def quick_sum(a, b):
    s = a + b
    return s, b - (s - a)


def unit(x):
    q = x * (2.0**23 + 1.0)
    return jnp.abs(q - q * (1.0 - 2.0**-24))


def pieces(x, sigma):
    s1 = (x + sigma) - sigma
    x = x - s1
    sigma = sigma * 2.0**-8
    s2 = (x + sigma) - sigma
    x = x - s2
    sigma = sigma * 2.0**-8
    s3 = (x + sigma) - sigma
    return s1.astype(BF16), s2.astype(BF16), s3.astype(BF16), (x - s3).astype(BF16)


def split3(x):
    a = x.astype(BF16)
    x = x - a.astype(F32)
    b = x.astype(BF16)
    return a, b, (x - b.astype(F32)).astype(BF16)


def tdot(a, b):
    return lax.dot_general(a, b, (((0,), (0,)), ((), ())), preferred_element_type=F32)


def dot(a, b, dims=((1,), (0,))):
    return lax.dot_general(a, b, (dims, ((), ())), precision=HIGHEST, preferred_element_type=F32)


def lane_sub():
    shape = (8, N)
    return lax.broadcasted_iota(jnp.int32, shape, 1), lax.broadcasted_iota(jnp.int32, shape, 0)


def fold(top, low, i):
    lane, sub = lane_sub()
    off = lane - 8 * i
    far = lane - 8 * (T - 1 - i)
    left = pltpu.roll(low, (8 * i + 8) % N, 1)
    block = pltpu.roll(low, (16 * i + 8) % N, 1)
    tile = jnp.where(off > sub, jnp.where(off < 8, block, left), top)
    diag = jnp.sum(jnp.where(far == sub, low, 0.0), axis=0, keepdims=True)
    return tile, diag


def unfold(tile, diag, i):
    lane, sub = lane_sub()
    off = lane - 8 * i
    far = lane - 8 * (T - 1 - i)
    top = jnp.where(off <= sub, tile, 0.0)
    left = pltpu.roll(tile, (N - 8 * i - 8) % N, 1)
    block = pltpu.roll(tile, (N - 16 * i - 8) % N, 1)
    low = jnp.where(far < 0, left, jnp.where(far == sub, diag, 0.0))
    upper = jnp.where((far > sub) & (far < 8), block, 0.0)
    return top, low, upper


def merge(slots):
    n = slots.shape[0]

    def pair(h, l, rows):
        hs, ls = slots[0, pl.ds(h, rows)], slots[0, pl.ds(l, rows)]
        for j in range(1, n):
            hs, e = two_sum(hs, slots[j, pl.ds(h, rows)])
            ls = ls + (slots[j, pl.ds(l, rows)] + e)
        return quick_sum(hs, ls)

    hi, lo = pair(HI, LO, 8)
    dh, dl = pair(DG, DG + 1, 1)
    co = slots[0, pl.ds(CO, 16)]
    for j in range(1, n):
        co = co + slots[j, pl.ds(CO, 16)]
    return hi, lo, co, dh, dl


def put(ref, parts):
    hi, lo, co, dh, dl = parts
    ref[pl.ds(HI, 8)] = hi
    ref[pl.ds(LO, 8)] = lo
    ref[pl.ds(CO, 16)] = co
    ref[pl.ds(DG, 1)] = dh
    ref[pl.ds(DG + 1, 1)] = dl


def sums_kernel(
    panel_hbm, next_hbm, out_ref,
    panel, nxt, ps, ns, first, got1, mine1, got2, mine2, got3, mine3, got4, in_sem, send_sem, recv_sem,
):
    rows = panel.shape[0]
    load_p = pltpu.make_async_copy(panel_hbm, panel, in_sem.at[0])
    load_n = pltpu.make_async_copy(next_hbm, nxt, in_sem.at[1])
    load_p.start()
    load_n.start()
    r, c = lax.axis_index("row"), lax.axis_index("col")
    y, x = lax.div(r, ROW_X), lax.rem(r, ROW_X)
    z, k = lax.div(c, COL_K), lax.rem(c, COL_K)
    g = x * COL_K + k

    def near(i):
        return (y * ROW_X + lax.div(i, COL_K), z * COL_K + lax.rem(i, COL_K))

    def along_z(i):
        return (r, i * COL_K + k)

    def along_y(i):
        return (i * ROW_X + x, c)

    groups = ((CHUNKS, g, near), (COL_Z, z, along_z), (ROW_Y, y, along_y))
    barrier = pltpu.get_barrier_semaphore()
    for n, me, at in groups:
        for j in range(1, n):
            pl.semaphore_signal(barrier, inc=1, device_id=at(lax.rem(me + j, n)), device_id_type=MESH)

    load_p.wait()
    block = 256
    def largest(i, m):
        v = jnp.abs(panel[pl.ds(pl.multiple_of(i * block, block), block), :])
        return jnp.maximum(m, jnp.max(v.reshape(block // 8, 8, N), axis=0))
    m = lax.fori_loop(0, rows // block, largest, jnp.zeros((8, N), F32))
    m = jnp.max(m, axis=0, keepdims=True)
    sigma = unit(m) * (1.5 * 2.0**17)

    def cut_p(i, _):
        at = pl.ds(pl.multiple_of(i * block, block), block)
        for j, s in enumerate(pieces(panel[at, :], sigma)):
            ps[at, pl.ds(j * N, N)] = s
        return 0
    lax.fori_loop(0, rows // block, cut_p, 0)
    load_n.wait()
    def cut_n(i, _):
        at = pl.ds(pl.multiple_of(i * block, block), block)
        for j, s in enumerate(split3(nxt[at, :])):
            ns[at, pl.ds(j * N, N)] = s
        return 0
    lax.fori_loop(0, rows // block, cut_n, 0)

    hi = lo = jnp.zeros((N, N), F32)
    low = cross = jnp.zeros((N, N), F32)
    step = 1024
    for i in range(0, rows, step):
        at = pl.ds(i, step)
        p12, p34 = ps[at, 0:2 * N], ps[at, 2 * N:4 * N]
        e = tdot(p12, p12)
        f = tdot(p12, p34)
        hi, err = two_sum(hi, e[:N, :N])
        lo = lo + err
        hi, err = two_sum(hi, e[:N, N:] + e[N:, :N])
        lo = lo + err + e[N:, N:]
        low = low + ((f[:N, :N] + f[:N, N:]) + (f[N:, :N] + f[N:, N:]))
        n12, n3 = ns[at, 0:2 * N], ns[at, 2 * N:3 * N]
        u = tdot(p12, n12)
        w = tdot(p34, n12)
        v = tdot(p12, n3)
        cross = cross + (u[:N, :N] + ((u[:N, N:] + u[N:, :N]) + (u[N:, N:] + w[:N, :N] + w[:N, N:] + w[N:, :N] + v[:N] + v[N:])))
    lo = lo + (low + low.T)
    hi, lo = quick_sum(hi, lo)
    for i in range(CHUNKS):
        a, b = slice(8 * i, 8 * i + 8), slice(8 * (T - 1 - i), 8 * (T - i))
        ht, hd = fold(hi[a], hi[b], i)
        lt, ld = fold(lo[a], lo[b], i)
        put(first.at[i], (ht, lt, cross[16 * i:16 * i + 16], hd, ld))

    pl.semaphore_wait(barrier, sum(n - 1 for n, _, _ in groups))

    def spread(phase, group, source, target):
        n, me, at = group
        for j in range(1, n):
            to = lax.rem(me + j, n)
            pltpu.make_async_remote_copy(
                source(to).at[pl.ds(0, USED)], target(j).at[pl.ds(0, USED)],
                send_sem.at[phase], recv_sem.at[phase], device_id=at(to), device_id_type=MESH,
            ).start()

    def arrived(sem, phase, n):
        whole = first.at[pl.ds(0, n - 1), pl.ds(0, USED)]
        pltpu.make_async_copy(whole, whole, sem.at[phase]).wait()

    spread(0, groups[0], lambda to: first.at[to], lambda j: got1.at[CHUNKS - j])
    got1[0] = first[g]
    arrived(recv_sem, 0, CHUNKS)
    put(mine1, merge(got1))
    spread(1, groups[1], lambda to: mine1, lambda j: got2.at[z])
    got2[z] = mine1[...]
    arrived(recv_sem, 1, COL_Z)
    put(mine2, merge(got2))
    spread(2, groups[2], lambda to: mine2, lambda j: got3.at[y])
    got3[y] = mine2[...]
    arrived(recv_sem, 2, ROW_Y)
    put(mine3, merge(got3))
    spread(3, groups[0], lambda to: mine3, lambda j: got4.at[g])
    got4[g] = mine3[...]
    arrived(recv_sem, 3, CHUNKS)
    out_ref[...] = got4[...]
    for phase, n in enumerate((CHUNKS, COL_Z, ROW_Y, CHUNKS)):
        arrived(send_sem, phase, n)


def lanes(v, i):
    return jnp.broadcast_to(v[:, i:i + 1], (8, N))


def subs(v, i):
    return jnp.broadcast_to(v[i:i + 1, :], (8, N))


def factor(gram, upper, lower_inv):
    lane, sub = lane_sub()
    a = [gram[8 * b:8 * b + 8, :] for b in range(T)]
    for b in range(T):
        off = lane - 8 * b
        inside = (off >= 0) & (off < 8)
        t = [lanes(a[b], 8 * b + i) for i in range(8)]
        v = jnp.where(inside, jnp.where(off == sub, 1.0, 0.0), a[b])
        g, h = [], {}
        pivots = jnp.ones((8, N), F32)
        for i in range(8):
            d = subs(t[i], i)
            inv = 1.0 / d
            pivots = jnp.where(sub == i, d, pivots)
            g.append(inv * subs(v, i))
            for j in range(i + 1, 8):
                h[i, j] = inv * subs(t[j], i)
            if i < 7:
                below = jnp.where(sub > i, t[i], 0.0)
                v = v - below * g[i]
                for j in range(i + 1, 8):
                    t[j] = t[j] - below * h[i, j]
        scale = lax.rsqrt(pivots)
        lower_inv[8 * b:8 * b + 8, :] = jnp.where(off < 8, v * scale, 0.0)
        u = v
        for j in range(8):
            u = jnp.where(off == j, jnp.where(sub <= j, t[j], 0.0), u)
        upper[8 * b:8 * b + 8, :] = jnp.where(off < 0, 0.0, u * scale)
        for b2 in range(b + 1, T):
            t2 = [lanes(a[b2], 8 * b + i) for i in range(8)]
            v2 = jnp.where(inside, 0.0, a[b2])
            for i in range(8):
                v2 = v2 - t2[i] * g[i]
                for j in range(i + 1, 8):
                    t2[j] = t2[j] - t2[i] * h[i, j]
            a[b2] = v2


def finish_kernel(
    sums, panel_hbm, next_hbm, q_hbm, r_ref, coupling_ref, trailing_hbm,
    panel, nxt, q, trail, hi_ref, lo_ref, gram, r1, x1, gram2, r2, x2, both, in_sem, out_sem, *, count,
):
    rows = panel.shape[0]
    load_p = pltpu.make_async_copy(panel_hbm, panel, in_sem.at[0])
    load_n = pltpu.make_async_copy(next_hbm, nxt, in_sem.at[1])
    load_p.start()
    load_n.start()
    for i in range(HALF):
        a, b = slice(8 * i, 8 * i + 8), slice(8 * (T - 1 - i), 8 * (T - i))
        for ref, at, dg in ((hi_ref, HI, DG), (lo_ref, LO, DG + 1)):
            top, low, up = unfold(sums[i, pl.ds(at, 8)], sums[i, pl.ds(dg, 1)], i)
            ref[0, a, :] = top
            ref[0, b, :] = low
            ref[1, a, :] = jnp.zeros_like(up)
            ref[1, b, :] = up
    row_id = lax.broadcasted_iota(jnp.int32, (N, N), 0)
    col_id = lax.broadcasted_iota(jnp.int32, (N, N), 1)

    def whole(ref):
        low = ref[0]
        up = ref[1]
        mirrored = jnp.where(col_id > row_id, (low + up.T).T, 0.0)
        return jnp.where(col_id > row_id, mirrored, low + up.T)

    hi, lo = whole(hi_ref) / count, whole(lo_ref) / count
    eye = row_id == col_id
    diag = jnp.where(eye, hi, 0.0)
    s_row = unit(lax.rsqrt(jnp.sum(diag, axis=0, keepdims=True)))
    s_col = unit(lax.rsqrt(jnp.sum(diag, axis=1, keepdims=True)))
    hi = hi * s_row * s_col
    lo = lo * s_row * s_col
    gram[...] = hi
    factor(gram, r1, x1)
    s1, s2, s3, s4 = pieces(r1[...], 1.5 * 2.0**15)
    p12, p34 = jnp.concatenate([s1, s2], 1), jnp.concatenate([s3, s4], 1)
    e = tdot(p12, p12)
    f = tdot(p12, p34)
    low = (f[:N, :N] + f[:N, N:]) + (f[N:, :N] + f[N:, N:])
    low = (low + low.T) + e[N:, N:]
    rest, e1 = two_sum(hi, -e[:N, :N])
    rest, e2 = two_sum(rest, -(e[:N, N:] + e[N:, :N]))
    rest = rest + ((e1 + e2) + (lo - low))
    x = x1[...]
    m = dot(x, r1[...], ((1,), (1,)))
    gram2[...] = dot(m, m, ((1,), (1,))) + dot(dot(x, rest), x, ((1,), (1,)))
    factor(gram2, r2, x2)
    r_ref[...] = dot(r2[...], r1[...]) / s_row
    w = dot(x, x2[...], ((0,), (1,))) * s_col
    cross = jnp.concatenate([sums[i, pl.ds(CO, 16)] for i in range(CHUNKS)], 0) / count
    coupling = dot(w, cross, ((0,), (0,)))
    coupling_ref[...] = coupling
    both[:, 0:N] = w
    both[:, N:2 * N] = dot(w, coupling)
    load_p.wait()
    load_n.wait()
    block = 256
    copies = []
    for i in range(0, rows, block):
        at = pl.ds(i, block)
        o = dot(panel[at, :], both[...])
        q[at, :] = o[:, :N]
        trail[at, :] = nxt[at, :] - o[:, N:]
        for src, dst, j in ((q, q_hbm, 0), (trail, trailing_hbm, 1)):
            copy = pltpu.make_async_copy(src.at[at], dst.at[at], out_sem.at[j, i // block])
            copy.start()
            copies.append(copy)
    for copy in copies:
        copy.wait()


def shards(panel, next_panel):
    rows = panel.shape[0]
    count = rows * lax.axis_size("row") * lax.axis_size("col")
    any_, vmem = pl.BlockSpec(memory_space=pl.ANY), pl.BlockSpec(memory_space=pltpu.VMEM)
    small = pltpu.VMEM((N, N), F32)
    tall = pltpu.VMEM((rows, N), F32)
    slots = pltpu.VMEM((CHUNKS, PADDED, N), F32)
    one = pltpu.VMEM((PADDED, N), F32)
    sums = pl.pallas_call(
        sums_kernel,
        name="sums",
        out_shape=jax.ShapeDtypeStruct((CHUNKS, PADDED, N), F32),
        in_specs=[any_, any_],
        out_specs=vmem,
        scratch_shapes=[
            tall, tall, pltpu.VMEM((rows, 4 * N), BF16), pltpu.VMEM((rows, 3 * N), BF16),
            slots, slots, one, slots, one, slots, one, slots,
            pltpu.SemaphoreType.DMA((2,)), pltpu.SemaphoreType.DMA((4,)), pltpu.SemaphoreType.DMA((4,)),
        ],
        compiler_params=pltpu.CompilerParams(collective_id=0, has_side_effects=True, vmem_limit_bytes=32 << 20),
    )(panel, next_panel)
    big = jax.ShapeDtypeStruct((rows, N), F32)
    little = jax.ShapeDtypeStruct((N, N), F32)
    q, r, coupling, trailing = pl.pallas_call(
        functools.partial(finish_kernel, count=count),
        name="finish",
        out_shape=(big, little, little, big),
        in_specs=[vmem, any_, any_],
        out_specs=(any_, vmem, vmem, any_),
        scratch_shapes=[
            tall, tall, tall, tall, pltpu.VMEM((2, N, N), F32), pltpu.VMEM((2, N, N), F32),
            small, small, small, small, small, small, pltpu.VMEM((N, 2 * N), F32),
            pltpu.SemaphoreType.DMA((2,)), pltpu.SemaphoreType.DMA((2, 8)),
        ],
        compiler_params=pltpu.CompilerParams(vmem_limit_bytes=32 << 20),
    )(sums, panel, next_panel)
    return q, r, coupling, trailing


def solution(mesh):
    return jax.shard_map(
        shards,
        mesh=mesh,
        in_specs=(P(("row", "col"), None), P(("row", "col"), None)),
        out_specs=(P(("row", "col"), None), P(), P(), P(("row", "col"), None)),
        check_vma=False,
    )
```

time: 848 us -> 53.2 us (0.06)
  waiting for transfers between devices: 768 us -> 0 us
  Pallas kernels: 0 us -> 49.9 us
  other arithmetic: 48.3 us -> 0 us
  matrix products: 14 us -> 0 us
  between operations: 13.9 us -> 0.65 us
    psum x3 -> x0, waiting for transfers between devices: 767 us -> none  [combine(): return lax.psum(stacked, ('row', 'col'))]
    pallas_call x0 -> x2, Pallas kernels: none -> 49.9 us  [the longest x1 35.7 us: shards(): pl.pallas_call(sums_kernel, name='sums', out_shape=jax.ShapeDtypeStruct((...]
    another operation x10 -> x0, other arithmetic: 45.7 us -> none  [the longest x6 24.8 us: factor(): lower = jnp.linalg.cholesky(gram)]
    dot_general x7 -> x0, matrix products: 13.5 us -> none  [the longest x4 6.96 us: times(): return jnp.dot(left, right, precision=lax.Precision.HIGHEST)]
  transfers between devices with their start and end apart: 3 -> 0, of which waited for: 3 -> 0; matrix products, arithmetic and copies ran while one was open for 0% -> 0% of each run, Pallas kernels for 0% -> 0%
where the time goes in v1:
time: 53.2 us; the launch traced here: 53 us
  Pallas kernels  49.9 us (94%)
  local copies, waits for them, and re-layouts  2.44 us (5%)
  between operations  0.65 us (1%)
    pallas_call x1, Pallas kernels, shards(): pl.pallas_call(sums_kernel, name='sums', out_shape=jax.ShapeDtypeStruct((...  35.7 us
    pallas_call x1, Pallas kernels, shards(): pl.pallas_call(functools.partial(finish_kernel, count=count), name='finis...  14.2 us
    unnamed x4, local copies, waits for them, and re-layouts  2.44 us

profile of v1, /device:TPU:1, one launch (start us, length us, event | category | flops | bytes accessed | tf_op | source)
XLA Modules:
  0.0 53.0 jit_solution(16909882390892336988)
XLA Ops:
  0.6 0.0 copy-start
  0.6 1.2 %copy-done = f32[2048,128]{1,0:T(8,128)S(1)} copy-done((f32[2048,128]{1,0:T(8,128)S(1)}, f32[2048,128]{1,0:T(8,128)}, u32[]{:S(2)}) %copy-start) | copy-done | bytes 1048600
  1.9 0.0 copy-start.1
  1.9 1.2 %copy-done.1 = f32[2048,128]{1,0:T(8,128)S(1)} copy-done((f32[2048,128]{1,0:T(8,128)S(1)}, f32[2048,128]{1,0:T(8,128)}, u32[]{:S(2)}) %copy-start.1) | copy-done | bytes 1048600
  3.1 35.7 %sums.1 = f32[8,40,128]{2,1,0:T(8,128)S(1)} custom-call(f32[2048,128]{1,0:T(8,128)S(1)} %copy-done, f32[2048,128]{1,0:T(8,128)S(1)} %copy-done.1), custom_call_target="tpu_custom_call" | custom-call | tf_op jit(solution)/shard_map/sums/pallas_call | solution.py:361
  38.8 14.2 %finish.1 = (f32[2048,128]{1,0:T(8,128)}, f32[128,128]{1,0:T(8,128)}, f32[128,128]{1,0:T(8,128)}, f32[2048,128]{1,0:T(8,128)}) custom-call(f32[8,40,128]{2,1,0:T(8,128)S(1)} %sums.1, f32[2048,128]{1,0:T(8,128)S(1)} %copy-done, f32[2048,128]{1,0:T(8,128)S(1)} %copy-done.1), custom_call_target="tpu_custom_call" | custom-call | tf_op jit(solution)/shard_map/finish/pallas_call | solution.py:376
Async XLA Ops:
  0.6 1.2 %copy-start = (f32[2048,128]{1,0:T(8,128)S(1)}, f32[2048,128]{1,0:T(8,128)}, u32[]{:S(2)}) copy-start(f32[2048,128]{1,0:T(8,128)} %panel_hbm.3) | copy-start | bytes 3145732
  1.9 1.2 %copy-start.1 = (f32[2048,128]{1,0:T(8,128)S(1)}, f32[2048,128]{1,0:T(8,128)}, u32[]{:S(2)}) copy-start(f32[2048,128]{1,0:T(8,128)} %next_hbm.3) | copy-start | bytes 3145732

commit v2 on v1

v2 whole, which is shorter than its diff:
```python
import functools

import jax
import jax.numpy as jnp
from jax import lax
from jax.experimental import pallas as pl
from jax.experimental.pallas import tpu as pltpu
from jax.sharding import PartitionSpec as P

MESH = pl.DeviceIdType.MESH
F32 = jnp.float32
BF16 = jnp.bfloat16
HIGHEST = lax.Precision.HIGHEST
N = 128
T = N // 8
HALF = T // 2
ROW_X = 4
ROW_Y = 8
COL_K = 2
COL_Z = 8
CHUNKS = ROW_X * COL_K
HI, LO, CO, DG, USED, PADDED = 0, 8, 16, 32, 34, 40


def two_sum(a, b):
    s = a + b
    t = s - a
    return s, (a - (s - t)) + (b - t)


def quick_sum(a, b):
    s = a + b
    return s, b - (s - a)


def unit(x):
    q = x * (2.0**23 + 1.0)
    return jnp.abs(q - q * (1.0 - 2.0**-24))


def pieces(x, sigma):
    s1 = (x + sigma) - sigma
    x = x - s1
    sigma = sigma * 2.0**-8
    s2 = (x + sigma) - sigma
    x = x - s2
    sigma = sigma * 2.0**-8
    s3 = (x + sigma) - sigma
    return s1.astype(BF16), s2.astype(BF16), s3.astype(BF16), (x - s3).astype(BF16)


def split3(x):
    a = x.astype(BF16)
    x = x - a.astype(F32)
    b = x.astype(BF16)
    return a, b, (x - b.astype(F32)).astype(BF16)


def tdot(a, b):
    return lax.dot_general(a, b, (((0,), (0,)), ((), ())), preferred_element_type=F32)


def dot(a, b, dims=((1,), (0,))):
    return lax.dot_general(a, b, (dims, ((), ())), precision=HIGHEST, preferred_element_type=F32)


def dot3(a, b, dims=((1,), (0,))):
    a1, b1 = a.astype(BF16), b.astype(BF16)
    a2, b2 = (a - a1.astype(F32)).astype(BF16), (b - b1.astype(F32)).astype(BF16)
    left = jnp.concatenate([a1, a1, a2], dims[0][0])
    right = jnp.concatenate([b1, b2, b1], dims[1][0])
    return lax.dot_general(left, right, (dims, ((), ())), preferred_element_type=F32)


def lane_sub():
    shape = (8, N)
    return lax.broadcasted_iota(jnp.int32, shape, 1), lax.broadcasted_iota(jnp.int32, shape, 0)


def fold(top, low, i):
    lane, sub = lane_sub()
    off = lane - 8 * i
    far = lane - 8 * (T - 1 - i)
    left = pltpu.roll(low, (8 * i + 8) % N, 1)
    block = pltpu.roll(low, (16 * i + 8) % N, 1)
    tile = jnp.where(off > sub, jnp.where(off < 8, block, left), top)
    diag = jnp.sum(jnp.where(far == sub, low, 0.0), axis=0, keepdims=True)
    return tile, diag


def unfold(tile, diag, i):
    lane, sub = lane_sub()
    off = lane - 8 * i
    far = lane - 8 * (T - 1 - i)
    top = jnp.where(off <= sub, tile, 0.0)
    left = pltpu.roll(tile, (N - 8 * i - 8) % N, 1)
    block = pltpu.roll(tile, (N - 16 * i - 8) % N, 1)
    low = jnp.where(far == sub, diag, jnp.where((far > sub) & (far < 8), block, 0.0))
    return top, jnp.where(far < 0, left, low)


def merge(slots):
    n = slots.shape[0]

    def pair(h, l, rows):
        hs, ls = slots[0, pl.ds(h, rows)], slots[0, pl.ds(l, rows)]
        for j in range(1, n):
            hs, e = two_sum(hs, slots[j, pl.ds(h, rows)])
            ls = ls + (slots[j, pl.ds(l, rows)] + e)
        return quick_sum(hs, ls)

    hi, lo = pair(HI, LO, 8)
    dh, dl = pair(DG, DG + 1, 1)
    co = slots[0, pl.ds(CO, 16)]
    for j in range(1, n):
        co = co + slots[j, pl.ds(CO, 16)]
    return hi, lo, co, dh, dl


def put(ref, parts):
    hi, lo, co, dh, dl = parts
    ref[pl.ds(HI, 8)] = hi
    ref[pl.ds(LO, 8)] = lo
    ref[pl.ds(CO, 16)] = co
    ref[pl.ds(DG, 1)] = dh
    ref[pl.ds(DG + 1, 1)] = dl


def sums_kernel(
    panel_hbm, next_hbm, out_ref,
    panel, nxt, ps, first, got1, mine1, got2, mine2, got3, mine3, got4, in_sem, send_sem, recv_sem,
):
    rows = panel.shape[0]
    step = 1024
    loads = []
    for i in range(0, rows, step):
        pair = []
        for j, (src, dst) in enumerate(((panel_hbm, panel), (next_hbm, nxt))):
            for h in range(2):
                at = pl.ds(i + h * (step // 2), step // 2)
                pair.append(pltpu.make_async_copy(src.at[at], dst.at[at], in_sem.at[j, 2 * (i // step) + h]))
                pair[-1].start()
        loads.append(pair)
    r, c = lax.axis_index("row"), lax.axis_index("col")
    y, x = lax.div(r, ROW_X), lax.rem(r, ROW_X)
    z, k = lax.div(c, COL_K), lax.rem(c, COL_K)
    g = x * COL_K + k

    def near(i):
        return (y * ROW_X + lax.div(i, COL_K), z * COL_K + lax.rem(i, COL_K))

    def along_z(i):
        return (r, i * COL_K + k)

    def along_y(i):
        return (i * ROW_X + x, c)

    groups = ((CHUNKS, g, near), (COL_Z, z, along_z), (ROW_Y, y, along_y))
    barrier = pltpu.get_barrier_semaphore()
    for n, me, at in groups:
        for j in range(1, n):
            pl.semaphore_signal(barrier, inc=1, device_id=at(lax.rem(me + j, n)), device_id_type=MESH)

    hi = lo = jnp.zeros((N, N), F32)
    low = cross = jnp.zeros((N, N), F32)
    block = 128
    for i in range(0, rows, step):
        for copy in loads[i // step]:
            copy.wait()
        m = jnp.zeros((8, N), F32)
        for j in range(0, step, block):
            v = jnp.abs(panel[pl.ds(i + j, block), :])
            m = jnp.maximum(m, jnp.max(v.reshape(block // 8, 8, N), axis=0))
        sigma = unit(jnp.max(m, axis=0, keepdims=True)) * (1.5 * 2.0**17)
        for j in range(0, step, block):
            at = pl.ds(i + j, block)
            for n, s in enumerate(pieces(panel[at, :], sigma) + split3(nxt[at, :])):
                ps[at, pl.ds(n * N, N)] = s
        at = pl.ds(i, step)
        e = tdot(ps[at, 0:2 * N], ps[at, :])
        w = tdot(ps[at, 2 * N:4 * N], ps[at, 4 * N:6 * N])
        hi, err = two_sum(hi, e[:N, :N])
        lo = lo + err
        hi, err = two_sum(hi, e[:N, N:2 * N] + e[N:, :N])
        lo = lo + err + e[N:, N:2 * N]
        low = low + ((e[:N, 2 * N:3 * N] + e[:N, 3 * N:4 * N]) + (e[N:, 2 * N:3 * N] + e[N:, 3 * N:4 * N]))
        part = (e[:N, 6 * N:] + e[N:, 6 * N:]) + ((w[:N, :N] + w[:N, N:]) + w[N:, :N])
        part = part + ((e[:N, 5 * N:6 * N] + e[N:, 4 * N:5 * N]) + e[N:, 5 * N:6 * N])
        cross = cross + (e[:N, 4 * N:5 * N] + part)
    lo = lo + (low + low.T)
    hi, lo = quick_sum(hi, lo)
    for i in range(CHUNKS):
        a, b = slice(8 * i, 8 * i + 8), slice(8 * (T - 1 - i), 8 * (T - i))
        ht, hd = fold(hi[a], hi[b], i)
        lt, ld = fold(lo[a], lo[b], i)
        put(first.at[i], (ht, lt, cross[16 * i:16 * i + 16], hd, ld))

    pl.semaphore_wait(barrier, sum(n - 1 for n, _, _ in groups))

    def spread(phase, group, source, target):
        n, me, at = group
        for j in range(1, n):
            to = lax.rem(me + j, n)
            pltpu.make_async_remote_copy(
                source(to).at[pl.ds(0, USED)], target(j).at[pl.ds(0, USED)],
                send_sem.at[phase], recv_sem.at[phase], device_id=at(to), device_id_type=MESH,
            ).start()

    def arrived(sem, phase, n):
        whole = first.at[pl.ds(0, n - 1), pl.ds(0, USED)]
        pltpu.make_async_copy(whole, whole, sem.at[phase]).wait()

    spread(0, groups[0], lambda to: first.at[to], lambda j: got1.at[CHUNKS - j])
    got1[0] = first[g]
    arrived(recv_sem, 0, CHUNKS)
    put(mine1, merge(got1))
    spread(1, groups[1], lambda to: mine1, lambda j: got2.at[z])
    got2[z] = mine1[...]
    arrived(recv_sem, 1, COL_Z)
    put(mine2, merge(got2))
    spread(2, groups[2], lambda to: mine2, lambda j: got3.at[y])
    got3[y] = mine2[...]
    arrived(recv_sem, 2, ROW_Y)
    put(mine3, merge(got3))
    spread(3, groups[0], lambda to: mine3, lambda j: got4.at[g])
    got4[g] = mine3[...]
    arrived(recv_sem, 3, CHUNKS)
    out_ref[...] = got4[...]
    for phase, n in enumerate((CHUNKS, COL_Z, ROW_Y, CHUNKS)):
        arrived(send_sem, phase, n)


def lanes(v, i):
    return jnp.broadcast_to(v[:, i:i + 1], (8, N))


def subs(v, i):
    return jnp.broadcast_to(v[i:i + 1, :], (8, N))


def factor(gram, upper, lower_inv):
    lane, sub = lane_sub()
    a = [gram[8 * b:8 * b + 8, :] for b in range(T)]
    t = [lanes(a[0], i) for i in range(8)]
    for b in range(T):
        off = lane - 8 * b
        inside = (off >= 0) & (off < 8)
        d = {(i, j): subs(t[j], i) for i in range(8) for j in range(i, 8)}
        rs, h = [], {}
        for i in range(8):
            rs.append(lax.rsqrt(d[i, i]))
            for j in range(i + 1, 8):
                h[i, j] = rs[i] * d[i, j]
            for k in range(i + 1, 8):
                for j in range(k, 8):
                    d[k, j] = d[k, j] - h[i, k] * h[i, j]
        ahead = f2 = None
        if b + 1 < T:
            ahead = [lanes(a[b + 1], 8 * (b + 1) + j) for j in range(8)]
            f2 = [lanes(a[b + 1], 8 * b + i) for i in range(8)]
            for i in range(8):
                f2[i] = f2[i] * rs[i]
                for j in range(i + 1, 8):
                    f2[j] = f2[j] - f2[i] * h[i, j]
                for j in range(8):
                    ahead[j] = ahead[j] - f2[i] * subs(f2[i], j)
        v = jnp.where(inside, jnp.where(off == sub, 1.0, 0.0), a[b])
        g = []
        scale = rs[0]
        for i in range(8):
            if i:
                scale = jnp.where(sub == i, rs[i], scale)
            g.append(rs[i] * subs(v, i))
            if i < 7:
                below = jnp.where(sub > i, t[i] * rs[i], 0.0)
                v = v - below * g[i]
                for j in range(i + 1, 8):
                    t[j] = t[j] - below * h[i, j]
        lower_inv[8 * b:8 * b + 8, :] = jnp.where(off < 8, v * scale, 0.0)
        u = v
        for j in range(8):
            u = jnp.where(off == j, jnp.where(sub <= j, t[j], 0.0), u)
        upper[8 * b:8 * b + 8, :] = jnp.where(off < 0, 0.0, u * scale)
        for b2 in range(b + 1, T):
            if b2 > b + 1:
                f2 = [lanes(a[b2], 8 * b + i) for i in range(8)]
            v2 = jnp.where(inside, 0.0, a[b2])
            for i in range(8):
                if b2 > b + 1:
                    f2[i] = f2[i] * rs[i]
                    for j in range(i + 1, 8):
                        f2[j] = f2[j] - f2[i] * h[i, j]
                v2 = v2 - f2[i] * g[i]
            a[b2] = v2
        t = ahead


def finish_kernel(
    sums, panel_hbm, next_hbm, q_hbm, r_ref, coupling_ref, trailing_hbm,
    panel, nxt, q, trail, hi_ref, lo_ref, gram, r1, x1, gram2, r2, x2, in_sem, out_sem, *, count,
):
    rows = panel.shape[0]
    block = 256
    loads = []
    for i in range(0, rows, block):
        at = pl.ds(i, block)
        for j, (src, dst) in enumerate(((panel_hbm, panel), (next_hbm, nxt))):
            loads.append(pltpu.make_async_copy(src.at[at], dst.at[at], in_sem.at[j, i // block]))
            loads[-1].start()
    for i in range(HALF):
        a, b = slice(8 * i, 8 * i + 8), slice(8 * (T - 1 - i), 8 * (T - i))
        for ref, at, dg in ((hi_ref, HI, DG), (lo_ref, LO, DG + 1)):
            ref[a, :], ref[b, :] = unfold(sums[i, pl.ds(at, 8)], sums[i, pl.ds(dg, 1)], i)
    row_id = lax.broadcasted_iota(jnp.int32, (N, N), 0)
    col_id = lax.broadcasted_iota(jnp.int32, (N, N), 1)
    eye = row_id == col_id

    def whole(ref):
        half = ref[...]
        return jnp.where(eye, half, half + half.T) * (1.0 / count)

    hi, lo = whole(hi_ref), whole(lo_ref)
    diag = jnp.where(eye, hi, 0.0)
    s_row = unit(lax.rsqrt(jnp.sum(diag, axis=0, keepdims=True)))
    s_col = unit(lax.rsqrt(jnp.sum(diag, axis=1, keepdims=True)))
    hi = hi * s_row * s_col
    lo = lo * s_row * s_col
    gram[...] = hi
    factor(gram, r1, x1)
    s1, s2, s3, s4 = pieces(r1[...], 1.5 * 2.0**15)
    p12, p34 = jnp.concatenate([s1, s2], 1), jnp.concatenate([s3, s4], 1)
    e = tdot(p12, jnp.concatenate([p12, p34], 1))
    low = (e[:N, 2 * N:3 * N] + e[:N, 3 * N:]) + (e[N:, 2 * N:3 * N] + e[N:, 3 * N:])
    low = (low + low.T) + e[N:, N:2 * N]
    rest, e1 = two_sum(hi, -e[:N, :N])
    rest, e2 = two_sum(rest, -(e[:N, N:2 * N] + e[N:, :N]))
    rest = rest + ((e1 + e2) + (lo - low))
    x = x1[...]
    m = dot(x, r1[...], ((1,), (1,)))
    y = dot3(x, rest)
    gram2[...] = dot(m, m, ((1,), (1,))) + dot3(y, x, ((1,), (1,)))
    factor(gram2, r2, x2)
    w = dot(x, x2[...], ((0,), (1,))) * s_col
    cross = jnp.concatenate([sums[i, pl.ds(CO, 16)] for i in range(CHUNKS)], 0) * (1.0 / count)
    coupling = dot(w, cross, ((0,), (0,)))
    coupling_ref[...] = coupling
    for copy in loads:
        copy.wait()
    copies = []

    def send(src, dst, j, i):
        at = pl.ds(i, block)
        copies.append(pltpu.make_async_copy(src.at[at], dst.at[at], out_sem.at[j, i // block]))
        copies[-1].start()

    for i in range(0, rows, block):
        q[pl.ds(i, block), :] = dot(panel[pl.ds(i, block), :], w)
        send(q, q_hbm, 0, i)
    back = dot(w, coupling)
    for i in range(0, rows, block):
        at = pl.ds(i, block)
        trail[at, :] = nxt[at, :] - dot(panel[at, :], back)
        send(trail, trailing_hbm, 1, i)
    r_ref[...] = dot(r2[...], r1[...]) / s_row
    for copy in copies:
        copy.wait()


def shards(panel, next_panel):
    rows = panel.shape[0]
    count = rows * lax.axis_size("row") * lax.axis_size("col")
    hbm, vmem = pl.BlockSpec(memory_space=pltpu.HBM), pl.BlockSpec(memory_space=pltpu.VMEM)
    small = pltpu.VMEM((N, N), F32)
    tall = pltpu.VMEM((rows, N), F32)
    slots = pltpu.VMEM((CHUNKS, PADDED, N), F32)
    one = pltpu.VMEM((PADDED, N), F32)
    sums = pl.pallas_call(
        sums_kernel,
        name="sums",
        out_shape=jax.ShapeDtypeStruct((CHUNKS, PADDED, N), F32),
        in_specs=[hbm, hbm],
        out_specs=vmem,
        scratch_shapes=[
            tall, tall, pltpu.VMEM((rows, 7 * N), BF16),
            slots, slots, one, slots, one, slots, one, slots,
            pltpu.SemaphoreType.DMA((2, 4)), pltpu.SemaphoreType.DMA((4,)), pltpu.SemaphoreType.DMA((4,)),
        ],
        compiler_params=pltpu.CompilerParams(collective_id=0, has_side_effects=True, vmem_limit_bytes=63 << 20),
    )(panel, next_panel)
    big = jax.ShapeDtypeStruct((rows, N), F32)
    little = jax.ShapeDtypeStruct((N, N), F32)
    q, r, coupling, trailing = pl.pallas_call(
        functools.partial(finish_kernel, count=count),
        name="finish",
        out_shape=(big, little, little, big),
        in_specs=[vmem, hbm, hbm],
        out_specs=(hbm, vmem, vmem, hbm),
        scratch_shapes=[
            tall, tall, tall, tall, small, small, small, small, small, small, small, small,
            pltpu.SemaphoreType.DMA((2, 8)), pltpu.SemaphoreType.DMA((2, 8)),
        ],
        compiler_params=pltpu.CompilerParams(vmem_limit_bytes=63 << 20),
    )(sums, panel, next_panel)
    return q, r, coupling, trailing


def solution(mesh):
    return jax.shard_map(
        shards,
        mesh=mesh,
        in_specs=(P(("row", "col"), None), P(("row", "col"), None)),
        out_specs=(P(("row", "col"), None), P(), P(), P(("row", "col"), None)),
        check_vma=False,
    )
```

time: 53.2 us -> 49.1 us (0.923)
  local copies, waits for them, and re-layouts: 2.44 us -> 0 us
  Pallas kernels: 49.9 us -> 48.3 us
    unnamed x4 -> x0, local copies, waits for them, and re-layouts: 2.44 us -> none
    pallas_call x1, Pallas kernels: 14.2 us -> 12 us  [shards(): pl.pallas_call(functools.partial(finish_kernel, count=count), name='finis...]
    pallas_call x1, Pallas kernels: 35.7 us -> 36.2 us  [shards(): pl.pallas_call(sums_kernel, name='sums', out_shape=jax.ShapeDtypeStruct((...]
where the time goes in v2:
time: 49.1 us; the launch traced here: 48.9 us
  Pallas kernels  48.3 us (98%)
  between operations  0.64 us (1%)
    pallas_call x1, Pallas kernels, shards(): pl.pallas_call(sums_kernel, name='sums', out_shape=jax.ShapeDtypeStruct((...  36.2 us
    pallas_call x1, Pallas kernels, shards(): pl.pallas_call(functools.partial(finish_kernel, count=count), name='finis...  12 us

profile of v2, /device:TPU:1, one launch (start us, length us, event | category | flops | bytes accessed | tf_op | source)
XLA Modules:
  0.0 48.9 jit_solution(12982861510191689942)
XLA Ops:
  0.6 36.2 %sums.1 = f32[8,40,128]{2,1,0:T(8,128)} custom-call(f32[2048,128]{1,0:T(8,128)} %panel_hbm.3, f32[2048,128]{1,0:T(8,128)} %next_hbm.3), custom_call_target="tpu_custom_call" | custom-call | tf_op jit(solution)/shard_map/sums/pallas_call | solution.py:377
  36.9 12.0 %finish.1 = (f32[2048,128]{1,0:T(8,128)}, f32[128,128]{1,0:T(8,128)}, f32[128,128]{1,0:T(8,128)}, f32[2048,128]{1,0:T(8,128)}) custom-call(f32[8,40,128]{2,1,0:T(8,128)} %sums.1, f32[2048,128]{1,0:T(8,128)} %panel_hbm.3, f32[2048,128]{1,0:T(8,128)} %next_hbm.3), custom_call_target="tpu_custom_call" | custom-call | tf_op jit(solution)/shard_map/finish/pallas_call | solution.py:392

commit v3 on v2

--- a/solution.py
+++ b/solution.py
@@ -19,7 +19,8 @@
 COL_K = 2
 COL_Z = 8
 CHUNKS = ROW_X * COL_K
-HI, LO, CO, DG, USED, PADDED = 0, 8, 16, 32, 34, 40
+HI, LO, DG, USED, PADDED = 0, 8, 16, 18, 24
+CROSS = N // CHUNKS
 
 
 def two_sum(a, b):
@@ -99,36 +100,29 @@
     return top, jnp.where(far < 0, left, low)
 
 
-def merge(slots):
-    n = slots.shape[0]
-
+def merge(slots, out):
     def pair(h, l, rows):
         hs, ls = slots[0, pl.ds(h, rows)], slots[0, pl.ds(l, rows)]
-        for j in range(1, n):
+        for j in range(1, slots.shape[0]):
             hs, e = two_sum(hs, slots[j, pl.ds(h, rows)])
             ls = ls + (slots[j, pl.ds(l, rows)] + e)
-        return quick_sum(hs, ls)
-
-    hi, lo = pair(HI, LO, 8)
-    dh, dl = pair(DG, DG + 1, 1)
-    co = slots[0, pl.ds(CO, 16)]
-    for j in range(1, n):
-        co = co + slots[j, pl.ds(CO, 16)]
-    return hi, lo, co, dh, dl
-
-
-def put(ref, parts):
-    hi, lo, co, dh, dl = parts
-    ref[pl.ds(HI, 8)] = hi
-    ref[pl.ds(LO, 8)] = lo
-    ref[pl.ds(CO, 16)] = co
-    ref[pl.ds(DG, 1)] = dh
-    ref[pl.ds(DG + 1, 1)] = dl
+        out[pl.ds(h, rows)], out[pl.ds(l, rows)] = quick_sum(hs, ls)
+
+    pair(HI, LO, 8)
+    pair(DG, DG + 1, 1)
+
+
+def plain_merge(slots, out):
+    total = slots[0]
+    for j in range(1, slots.shape[0]):
+        total = total + slots[j]
+    out[...] = total
 
 
 def sums_kernel(
-    panel_hbm, next_hbm, out_ref,
-    panel, nxt, ps, first, got1, mine1, got2, mine2, got3, mine3, got4, in_sem, send_sem, recv_sem,
+    panel_hbm, next_hbm, gram_ref, cross_ref, panel, nxt, ps,
+    gram0, gram1, gram2, gram3, gram4, own1, own2, own3,
+    cross0, cross1, cross2, cross3, cross4, part1, part2, part3, in_sem, send_sem, recv_sem,
 ):
     rows = panel.shape[0]
     step = 1024
@@ -162,10 +156,10 @@
             pl.semaphore_signal(barrier, inc=1, device_id=at(lax.rem(me + j, n)), device_id_type=MESH)
 
     hi = lo = jnp.zeros((N, N), F32)
-    low = cross = jnp.zeros((N, N), F32)
+    low = jnp.zeros((N, N), F32)
     block = 128
     for i in range(0, rows, step):
-        for copy in loads[i // step]:
+        for copy in loads[i // step][:2]:
             copy.wait()
         m = jnp.zeros((8, N), F32)
         for j in range(0, step, block):
@@ -174,60 +168,88 @@
         sigma = unit(jnp.max(m, axis=0, keepdims=True)) * (1.5 * 2.0**17)
         for j in range(0, step, block):
             at = pl.ds(i + j, block)
-            for n, s in enumerate(pieces(panel[at, :], sigma) + split3(nxt[at, :])):
+            for n, s in enumerate(pieces(panel[at, :], sigma)):
                 ps[at, pl.ds(n * N, N)] = s
         at = pl.ds(i, step)
-        e = tdot(ps[at, 0:2 * N], ps[at, :])
-        w = tdot(ps[at, 2 * N:4 * N], ps[at, 4 * N:6 * N])
+        e = tdot(ps[at, 0:2 * N], ps[at, 0:4 * N])
         hi, err = two_sum(hi, e[:N, :N])
         lo = lo + err
         hi, err = two_sum(hi, e[:N, N:2 * N] + e[N:, :N])
         lo = lo + err + e[N:, N:2 * N]
         low = low + ((e[:N, 2 * N:3 * N] + e[:N, 3 * N:4 * N]) + (e[N:, 2 * N:3 * N] + e[N:, 3 * N:4 * N]))
-        part = (e[:N, 6 * N:] + e[N:, 6 * N:]) + ((w[:N, :N] + w[:N, N:]) + w[N:, :N])
-        part = part + ((e[:N, 5 * N:6 * N] + e[N:, 4 * N:5 * N]) + e[N:, 5 * N:6 * N])
-        cross = cross + (e[:N, 4 * N:5 * N] + part)
     lo = lo + (low + low.T)
     hi, lo = quick_sum(hi, lo)
     for i in range(CHUNKS):
         a, b = slice(8 * i, 8 * i + 8), slice(8 * (T - 1 - i), 8 * (T - i))
         ht, hd = fold(hi[a], hi[b], i)
         lt, ld = fold(lo[a], lo[b], i)
-        put(first.at[i], (ht, lt, cross[16 * i:16 * i + 16], hd, ld))
+        gram0[i, pl.ds(HI, 8)] = ht
+        gram0[i, pl.ds(LO, 8)] = lt
+        gram0[i, pl.ds(DG, 1)] = hd
+        gram0[i, pl.ds(DG + 1, 1)] = ld
 
     pl.semaphore_wait(barrier, sum(n - 1 for n, _, _ in groups))
 
-    def spread(phase, group, source, target):
+    def spread(stream, phase, group, source, target, used):
         n, me, at = group
         for j in range(1, n):
             to = lax.rem(me + j, n)
             pltpu.make_async_remote_copy(
-                source(to).at[pl.ds(0, USED)], target(j).at[pl.ds(0, USED)],
-                send_sem.at[phase], recv_sem.at[phase], device_id=at(to), device_id_type=MESH,
+                source(to).at[pl.ds(0, used)], target(j).at[pl.ds(0, used)],
+                send_sem.at[stream, phase], recv_sem.at[stream, phase], device_id=at(to), device_id_type=MESH,
             ).start()
 
-    def arrived(sem, phase, n):
-        whole = first.at[pl.ds(0, n - 1), pl.ds(0, USED)]
-        pltpu.make_async_copy(whole, whole, sem.at[phase]).wait()
-
-    spread(0, groups[0], lambda to: first.at[to], lambda j: got1.at[CHUNKS - j])
-    got1[0] = first[g]
-    arrived(recv_sem, 0, CHUNKS)
-    put(mine1, merge(got1))
-    spread(1, groups[1], lambda to: mine1, lambda j: got2.at[z])
-    got2[z] = mine1[...]
-    arrived(recv_sem, 1, COL_Z)
-    put(mine2, merge(got2))
-    spread(2, groups[2], lambda to: mine2, lambda j: got3.at[y])
-    got3[y] = mine2[...]
-    arrived(recv_sem, 2, ROW_Y)
-    put(mine3, merge(got3))
-    spread(3, groups[0], lambda to: mine3, lambda j: got4.at[g])
-    got4[g] = mine3[...]
-    arrived(recv_sem, 3, CHUNKS)
-    out_ref[...] = got4[...]
-    for phase, n in enumerate((CHUNKS, COL_Z, ROW_Y, CHUNKS)):
-        arrived(send_sem, phase, n)
+    def arrived(sem, stream, phase, n):
+        whole = (gram0.at[pl.ds(0, n - 1), pl.ds(0, USED)], cross0.at[pl.ds(0, n - 1)])[stream]
+        pltpu.make_async_copy(whole, whole, sem.at[stream, phase]).wait()
+
+    class Stream:
+        def __init__(self, stream, first, slots, own, add, used):
+            self.stream, self.first, self.slots, self.own, self.add, self.used = stream, first, slots, own, add, used
+
+        def scatter(self):
+            spread(self.stream, 0, groups[0], lambda to: self.first.at[to], lambda j: self.slots[0].at[CHUNKS - j], self.used)
+            self.slots[0][0] = self.first[g]
+
+        def forward(self, phase):
+            group = groups[(phase + 1) % 3]
+            slot = group[1]
+            arrived(recv_sem, self.stream, phase, groups[phase][0])
+            own = self.own[phase]
+            self.add(self.slots[phase], own)
+            spread(self.stream, phase + 1, group, lambda to: own, lambda j: self.slots[phase + 1].at[slot], self.used)
+            self.slots[phase + 1][slot] = own[...]
+
+    gram = Stream(0, gram0, (gram1, gram2, gram3, gram4), (own1, own2, own3), merge, USED)
+    cross = Stream(1, cross0, (cross1, cross2, cross3, cross4), (part1, part2, part3), plain_merge, CROSS)
+    gram.scatter()
+    total = jnp.zeros((N, N), F32)
+    for i in range(0, rows, step):
+        for copy in loads[i // step][2:]:
+            copy.wait()
+        for j in range(0, step, block):
+            at = pl.ds(i + j, block)
+            for n, s in enumerate(split3(nxt[at, :])):
+                ps[at, pl.ds((4 + n) * N, N)] = s
+        at = pl.ds(i, step)
+        e = tdot(ps[at, 0:2 * N], ps[at, 4 * N:7 * N])
+        w = tdot(ps[at, 2 * N:4 * N], ps[at, 4 * N:6 * N])
+        part = (e[:N, 2 * N:] + e[N:, 2 * N:]) + ((w[:N, :N] + w[:N, N:]) + w[N:, :N])
+        part = part + ((e[:N, N:2 * N] + e[N:, :N]) + e[N:, N:2 * N])
+        total = total + (e[:N, :N] + part)
+    for i in range(CHUNKS):
+        cross0[i] = total[CROSS * i:CROSS * (i + 1)]
+    cross.scatter()
+    for phase in range(3):
+        gram.forward(phase)
+        cross.forward(phase)
+    arrived(recv_sem, 0, 3, CHUNKS)
+    gram_ref[...] = gram4[...]
+    arrived(recv_sem, 1, 3, CHUNKS)
+    cross_ref[...] = cross4[...]
+    for stream in range(2):
+        for phase, n in enumerate((CHUNKS, COL_Z, ROW_Y, CHUNKS)):
+            arrived(send_sem, stream, phase, n)
 
 
 def lanes(v, i):
@@ -296,7 +318,7 @@
 
 
 def finish_kernel(
-    sums, panel_hbm, next_hbm, q_hbm, r_ref, coupling_ref, trailing_hbm,
+    sums, cross_sum, panel_hbm, next_hbm, q_hbm, r_ref, coupling_ref, trailing_hbm,
     panel, nxt, q, trail, hi_ref, lo_ref, gram, r1, x1, gram2, r2, x2, in_sem, out_sem, *, count,
 ):
     rows = panel.shape[0]
@@ -341,7 +363,7 @@
     gram2[...] = dot(m, m, ((1,), (1,))) + dot3(y, x, ((1,), (1,)))
     factor(gram2, r2, x2)
     w = dot(x, x2[...], ((0,), (1,))) * s_col
-    cross = jnp.concatenate([sums[i, pl.ds(CO, 16)] for i in range(CHUNKS)], 0) * (1.0 / count)
+    cross = cross_sum[...].reshape(N, N) * (1.0 / count)
     coupling = dot(w, cross, ((0,), (0,)))
     coupling_ref[...] = coupling
     for copy in loads:
@@ -374,18 +396,20 @@
     tall = pltpu.VMEM((rows, N), F32)
     slots = pltpu.VMEM((CHUNKS, PADDED, N), F32)
     one = pltpu.VMEM((PADDED, N), F32)
-    sums = pl.pallas_call(
+    cross_slots = pltpu.VMEM((CHUNKS, CROSS, N), F32)
+    cross_one = pltpu.VMEM((CROSS, N), F32)
+    gram, cross = pl.pallas_call(
         sums_kernel,
         name="sums",
-        out_shape=jax.ShapeDtypeStruct((CHUNKS, PADDED, N), F32),
+        out_shape=(jax.ShapeDtypeStruct((CHUNKS, PADDED, N), F32), jax.ShapeDtypeStruct((CHUNKS, CROSS, N), F32)),
         in_specs=[hbm, hbm],
-        out_specs=vmem,
+        out_specs=(vmem, vmem),
         scratch_shapes=[
             tall, tall, pltpu.VMEM((rows, 7 * N), BF16),
-            slots, slots, one, slots, one, slots, one, slots,
-            pltpu.SemaphoreType.DMA((2, 4)), pltpu.SemaphoreType.DMA((4,)), pltpu.SemaphoreType.DMA((4,)),
+            *(slots,) * 5, *(one,) * 3, *(cross_slots,) * 5, *(cross_one,) * 3,
+            pltpu.SemaphoreType.DMA((2, 4)), pltpu.SemaphoreType.DMA((2, 4)), pltpu.SemaphoreType.DMA((2, 4)),
         ],
-        compiler_params=pltpu.CompilerParams(collective_id=0, has_side_effects=True, vmem_limit_bytes=63 << 20),
+        compiler_params=pltpu.CompilerParams(collective_id=0, has_side_effects=True, vmem_limit_bytes=53 << 20),
     )(panel, next_panel)
     big = jax.ShapeDtypeStruct((rows, N), F32)
     little = jax.ShapeDtypeStruct((N, N), F32)
@@ -393,14 +417,14 @@
         functools.partial(finish_kernel, count=count),
         name="finish",
         out_shape=(big, little, little, big),
-        in_specs=[vmem, hbm, hbm],
+        in_specs=[vmem, vmem, hbm, hbm],
         out_specs=(hbm, vmem, vmem, hbm),
         scratch_shapes=[
             tall, tall, tall, tall, small, small, small, small, small, small, small, small,
             pltpu.SemaphoreType.DMA((2, 8)), pltpu.SemaphoreType.DMA((2, 8)),
         ],
-        compiler_params=pltpu.CompilerParams(vmem_limit_bytes=63 << 20),
-    )(sums, panel, next_panel)
+        compiler_params=pltpu.CompilerParams(vmem_limit_bytes=53 << 20),
+    )(gram, cross, panel, next_panel)
     return q, r, coupling, trailing
 
 

time: 49.1 us -> 47.3 us (0.963)
  Pallas kernels: 48.3 us -> 46.5 us
    pallas_call x1, Pallas kernels: 36.2 us -> 34.1 us  [shards(): pl.pallas_call(sums_kernel, name='sums', out_shape=(jax.ShapeDtypeStruct(...]
where the time goes in v3:
time: 47.3 us; the launch traced here: 47.2 us
  Pallas kernels  46.5 us (98%)
  between operations  0.64 us (1%)
    pallas_call x1, Pallas kernels, shards(): pl.pallas_call(sums_kernel, name='sums', out_shape=(jax.ShapeDtypeStruct(...  34.1 us
    pallas_call x1, Pallas kernels, shards(): pl.pallas_call(functools.partial(finish_kernel, count=count), name='finis...  12.4 us

profile of v3, /device:TPU:1, one launch (start us, length us, event | category | flops | bytes accessed | tf_op | source)
XLA Modules:
  0.0 47.2 jit_solution(2651282133007466093)
XLA Ops:
  0.6 34.1 %sums.1 = (f32[8,24,128]{2,1,0:T(8,128)S(1)}, f32[8,16,128]{2,1,0:T(8,128)S(1)}) custom-call(f32[2048,128]{1,0:T(8,128)} %panel_hbm.3, f32[2048,128]{1,0:T(8,128)} %next_hbm.3), custom_call_target="tpu_custom_call" | custom-call | tf_op jit(solution)/shard_map/sums/pallas_call | solution.py:401
  34.7 12.4 %finish.1 = (f32[2048,128]{1,0:T(8,128)}, f32[128,128]{1,0:T(8,128)}, f32[128,128]{1,0:T(8,128)}, f32[2048,128]{1,0:T(8,128)}) custom-call(f32[8,24,128]{2,1,0:T(8,128)S(1)} %get-tuple-element.6.sums, f32[8,16,128]{2,1,0:T(8,128)S(1)} %get-tuple-element.7.cross_sum, f32[2048,128]{1,0:T(8,128)} %panel_hbm.3, f32[2048,128]{1,0:T(8,128)} %next_hbm.3), custom_call_target="tpu_custom_call" | custom-call | tf_op jit(solution)/shard_map/finish/pallas_call | solution.py:416

commit v4 on v3

--- a/solution.py
+++ b/solution.py
@@ -73,6 +73,18 @@
     return lax.dot_general(left, right, (dims, ((), ())), preferred_element_type=F32)
 
 
+def weights(w):
+    a, b, c = split3(w)
+    ab = jnp.concatenate([a, b], 1)
+    return jnp.concatenate([ab, ab], 0), jnp.concatenate([c, a], 0)
+
+
+def tall_dot(cut, pair):
+    a = jnp.dot(cut[:, 0:2 * N], pair[0], preferred_element_type=F32)
+    b = jnp.dot(cut[:, N:3 * N], pair[1], preferred_element_type=F32)
+    return a[:, :N] + (a[:, N:] + b)
+
+
 def lane_sub():
     shape = (8, N)
     return lax.broadcasted_iota(jnp.int32, shape, 1), lax.broadcasted_iota(jnp.int32, shape, 0)
@@ -126,15 +138,13 @@
 ):
     rows = panel.shape[0]
     step = 1024
-    loads = []
-    for i in range(0, rows, step):
-        pair = []
-        for j, (src, dst) in enumerate(((panel_hbm, panel), (next_hbm, nxt))):
+    loads = [[] for _ in range(0, rows, step)]
+    for j, (src, dst) in enumerate(((panel_hbm, panel), (next_hbm, nxt))):
+        for i in range(0, rows, step):
             for h in range(2):
                 at = pl.ds(i + h * (step // 2), step // 2)
-                pair.append(pltpu.make_async_copy(src.at[at], dst.at[at], in_sem.at[j, 2 * (i // step) + h]))
-                pair[-1].start()
-        loads.append(pair)
+                loads[i // step].append(pltpu.make_async_copy(src.at[at], dst.at[at], in_sem.at[j, 2 * (i // step) + h]))
+                loads[i // step][-1].start()
     r, c = lax.axis_index("row"), lax.axis_index("col")
     y, x = lax.div(r, ROW_X), lax.rem(r, ROW_X)
     z, k = lax.div(c, COL_K), lax.rem(c, COL_K)
@@ -192,7 +202,7 @@
 
     def spread(stream, phase, group, source, target, used):
         n, me, at = group
-        for j in range(1, n):
+        for j in sorted(range(1, n), key=lambda j: abs(2 * j - n)):
             to = lax.rem(me + j, n)
             pltpu.make_async_remote_copy(
                 source(to).at[pl.ds(0, used)], target(j).at[pl.ds(0, used)],
@@ -319,7 +329,7 @@
 
 def finish_kernel(
     sums, cross_sum, panel_hbm, next_hbm, q_hbm, r_ref, coupling_ref, trailing_hbm,
-    panel, nxt, q, trail, hi_ref, lo_ref, gram, r1, x1, gram2, r2, x2, in_sem, out_sem, *, count,
+    panel, nxt, q, trail, cut, hi_ref, lo_ref, gram, r1, x1, gram2, r2, x2, in_sem, out_sem, *, count,
 ):
     rows = panel.shape[0]
     block = 256
@@ -366,6 +376,7 @@
     cross = cross_sum[...].reshape(N, N) * (1.0 / count)
     coupling = dot(w, cross, ((0,), (0,)))
     coupling_ref[...] = coupling
+    pair = weights(w)
     for copy in loads:
         copy.wait()
     copies = []
@@ -376,12 +387,15 @@
         copies[-1].start()
 
     for i in range(0, rows, block):
-        q[pl.ds(i, block), :] = dot(panel[pl.ds(i, block), :], w)
+        at = pl.ds(i, block)
+        first, second, third = split3(panel[at, :])
+        cut[at, :] = jnp.concatenate([second, first, third], 1)
+        q[at, :] = tall_dot(cut[at, :], pair)
         send(q, q_hbm, 0, i)
-    back = dot(w, coupling)
+    back = weights(dot(w, coupling))
     for i in range(0, rows, block):
         at = pl.ds(i, block)
-        trail[at, :] = nxt[at, :] - dot(panel[at, :], back)
+        trail[at, :] = nxt[at, :] - tall_dot(cut[at, :], back)
         send(trail, trailing_hbm, 1, i)
     r_ref[...] = dot(r2[...], r1[...]) / s_row
     for copy in copies:
@@ -420,7 +434,7 @@
         in_specs=[vmem, vmem, hbm, hbm],
         out_specs=(hbm, vmem, vmem, hbm),
         scratch_shapes=[
-            tall, tall, tall, tall, small, small, small, small, small, small, small, small,
+            tall, tall, tall, tall, pltpu.VMEM((rows, 3 * N), BF16), small, small, small, small, small, small, small, small,
             pltpu.SemaphoreType.DMA((2, 8)), pltpu.SemaphoreType.DMA((2, 8)),
         ],
         compiler_params=pltpu.CompilerParams(vmem_limit_bytes=53 << 20),

time: 47.3 us -> 46.5 us (0.983)
  Pallas kernels: 46.5 us -> 45.6 us
    pallas_call x1, Pallas kernels: 34.1 us -> 33.6 us  [shards(): pl.pallas_call(sums_kernel, name='sums', out_shape=(jax.ShapeDtypeStruct(...]
where the time goes in v4:
time: 46.5 us; the launch traced here: 46.3 us
  Pallas kernels  45.6 us (98%)
  between operations  0.64 us (1%)
    pallas_call x1, Pallas kernels, shards(): pl.pallas_call(sums_kernel, name='sums', out_shape=(jax.ShapeDtypeStruct(...  33.6 us
    pallas_call x1, Pallas kernels, shards(): pl.pallas_call(functools.partial(finish_kernel, count=count), name='finis...  12 us

profile of v4, /device:TPU:1, one launch (start us, length us, event | category | flops | bytes accessed | tf_op | source)
XLA Modules:
  0.0 46.3 jit_solution(18193654717505656066)
XLA Ops:
  0.6 33.6 %sums.1 = (f32[8,24,128]{2,1,0:T(8,128)S(1)}, f32[8,16,128]{2,1,0:T(8,128)S(1)}) custom-call(f32[2048,128]{1,0:T(8,128)} %panel_hbm.3, f32[2048,128]{1,0:T(8,128)} %next_hbm.3), custom_call_target="tpu_custom_call" | custom-call | tf_op jit(solution)/shard_map/sums/pallas_call | solution.py:415
  34.2 12.0 %finish.1 = (f32[2048,128]{1,0:T(8,128)}, f32[128,128]{1,0:T(8,128)}, f32[128,128]{1,0:T(8,128)}, f32[2048,128]{1,0:T(8,128)}) custom-call(f32[8,24,128]{2,1,0:T(8,128)S(1)} %get-tuple-element.6.sums, f32[8,16,128]{2,1,0:T(8,128)S(1)} %get-tuple-element.7.cross_sum, f32[2048,128]{1,0:T(8,128)} %panel_hbm.3, f32[2048,128]{1,0:T(8,128)} %next_hbm.3), custom_call_target="tpu_custom_call" | custom-call | tf_op jit(solution)/shard_map/finish/pallas_call | solution.py:430

commit v5 on v4

--- a/solution.py
+++ b/solution.py
@@ -333,12 +333,12 @@
 ):
     rows = panel.shape[0]
     block = 256
-    loads = []
-    for i in range(0, rows, block):
-        at = pl.ds(i, block)
-        for j, (src, dst) in enumerate(((panel_hbm, panel), (next_hbm, nxt))):
-            loads.append(pltpu.make_async_copy(src.at[at], dst.at[at], in_sem.at[j, i // block]))
-            loads[-1].start()
+    loads = [
+        pltpu.make_async_copy(panel_hbm, panel, in_sem.at[0, 0]),
+        pltpu.make_async_copy(next_hbm, nxt, in_sem.at[1, 0]),
+    ]
+    for copy in loads:
+        copy.start()
     for i in range(HALF):
         a, b = slice(8 * i, 8 * i + 8), slice(8 * (T - 1 - i), 8 * (T - i))
         for ref, at, dg in ((hi_ref, HI, DG), (lo_ref, LO, DG + 1)):
@@ -371,14 +371,22 @@
     m = dot(x, r1[...], ((1,), (1,)))
     y = dot3(x, rest)
     gram2[...] = dot(m, m, ((1,), (1,))) + dot3(y, x, ((1,), (1,)))
-    factor(gram2, r2, x2)
-    w = dot(x, x2[...], ((0,), (1,))) * s_col
-    cross = cross_sum[...].reshape(N, N) * (1.0 / count)
-    coupling = dot(w, cross, ((0,), (0,)))
-    coupling_ref[...] = coupling
-    pair = weights(w)
+    cross = dot(x, cross_sum[...].reshape(N, N) * (1.0 / count) * s_col)
+    pair = weights((x * s_row).T)
     for copy in loads:
         copy.wait()
+
+    def pieces_of(v):
+        first, second, third = split3(v)
+        return jnp.concatenate([second, first, third], 1)
+
+    for i in range(0, rows, block):
+        at = pl.ds(i, block)
+        cut[at, :] = pieces_of(tall_dot(pieces_of(panel[at, :]), pair))
+    factor(gram2, r2, x2)
+    coupling = dot(x2[...], cross)
+    coupling_ref[...] = coupling
+    pair = weights(x2[...].T)
     copies = []
 
     def send(src, dst, j, i):
@@ -388,11 +396,9 @@
 
     for i in range(0, rows, block):
         at = pl.ds(i, block)
-        first, second, third = split3(panel[at, :])
-        cut[at, :] = jnp.concatenate([second, first, third], 1)
         q[at, :] = tall_dot(cut[at, :], pair)
         send(q, q_hbm, 0, i)
-    back = weights(dot(w, coupling))
+    back = weights(dot(x2[...], coupling, ((0,), (0,))))
     for i in range(0, rows, block):
         at = pl.ds(i, block)
         trail[at, :] = nxt[at, :] - tall_dot(cut[at, :], back)

time: 46.5 us -> 46.5 us (level)
  no operation moved by 1% of the time
where the time goes in v5:
time: 46.5 us; the launch traced here: 46.3 us
  Pallas kernels  45.7 us (98%)
  between operations  0.64 us (1%)
    pallas_call x1, Pallas kernels, shards(): pl.pallas_call(sums_kernel, name='sums', out_shape=(jax.ShapeDtypeStruct(...  33.6 us
    pallas_call x1, Pallas kernels, shards(): pl.pallas_call(functools.partial(finish_kernel, count=count), name='finis...  12.1 us

profile of v5, /device:TPU:1, one launch (start us, length us, event | category | flops | bytes accessed | tf_op | source)
XLA Modules:
  0.0 46.3 jit_solution(3471331720651598184)
XLA Ops:
  0.6 33.6 %sums.1 = (f32[8,24,128]{2,1,0:T(8,128)S(1)}, f32[8,16,128]{2,1,0:T(8,128)S(1)}) custom-call(f32[2048,128]{1,0:T(8,128)} %panel_hbm.3, f32[2048,128]{1,0:T(8,128)} %next_hbm.3), custom_call_target="tpu_custom_call" | custom-call | tf_op jit(solution)/shard_map/sums/pallas_call | solution.py:421
  34.2 12.1 %finish.1 = (f32[2048,128]{1,0:T(8,128)}, f32[128,128]{1,0:T(8,128)}, f32[128,128]{1,0:T(8,128)}, f32[2048,128]{1,0:T(8,128)}) custom-call(f32[8,24,128]{2,1,0:T(8,128)S(1)} %get-tuple-element.6.sums, f32[8,16,128]{2,1,0:T(8,128)S(1)} %get-tuple-element.7.cross_sum, f32[2048,128]{1,0:T(8,128)} %panel_hbm.3, f32[2048,128]{1,0:T(8,128)} %next_hbm.3), custom_call_target="tpu_custom_call" | custom-call | tf_op jit(solution)/shard_map/finish/pallas_call | solution.py:436
